TPU v7x, 512 devices: a whole 4x4x16 slice. The times are simulated.
512 devices in a mesh: replica: 32 (over y, x, core), tensor: 16 (over z).
Axes of the slice: x: 4, y: 4, z: 16, core: 2. Of those that a mesh axis runs over, the one named last changes fastest.
Arguments:
- tokens: bfloat16 [16384, 8192], P('replica', 'tensor'), may hold values from -6 to 6
- cotangent: bfloat16 [16384, 512], P(('replica', 'tensor')), may hold values from -6 to 6
- drift: bfloat16 [32, 512, 8192], P('replica', None, 'tensor'), may hold values from -8 to 8
- error: bfloat16 [32, 512, 8192], P('replica', None, 'tensor'), may hold values from -3 to 3
- weight: float32 [512, 8192], P('replica', 'tensor'), may hold values from -6 to 6
- momentum: float32 [512, 8192], P('replica', 'tensor'), may hold values from -3 to 3
- factor: float32 [32, 8192], P(None, 'tensor'), may hold values from -6 to 6
- gain: float32 [128], replicated, may hold values from 0.1 to 1.9
Outputs:
- new_weight: float32 [512, 8192], P('replica', 'tensor')
- new_momentum: float32 [512, 8192], P('replica', 'tensor')
- new_error: bfloat16 [32, 512, 8192], P('replica', None, 'tensor')
- new_factor: float32 [32, 8192], P(None, 'tensor')
- weight_grad: bfloat16 [32, 512, 8192], P('replica', None, 'tensor')
All inputs are finite; a program needn't handle non-finite values.
Results may differ from a plain program's by a relative error of at most 0.015.
Values may be sent and summed in bfloat16 or wider, within the bound.
A program may use at most 64 MiB of HBM per device.

v0:
```python
import math

import jax
import jax.numpy as jnp
from jax import lax
from jax.sharding import PartitionSpec as P

highest = lax.Precision.HIGHEST
outer_rate = 0.7
outer_beta = 0.9


def contract(left, right, left_dim, right_dim):
    return lax.dot_general(
        left,
        right,
        (((left_dim,), (right_dim,)), ((), ())),
        precision=highest,
        preferred_element_type=jnp.float32,
    )


def factor_basis(left):
    gram = contract(left, left, 1, 1)
    shift = 0.001 * jnp.trace(gram) / left.shape[0] + 1e-06
    lower = jnp.linalg.cholesky(gram + shift * jnp.eye(left.shape[0], dtype=jnp.float32))
    return (lower, jax.scipy.linalg.solve_triangular(lower, left, lower=True))


def key_grad(keys, cotangent, gain):
    count = keys.shape[0]
    width = gain.shape[0]
    shaped = keys.reshape(count, -1, width)
    weighted = gain * cotangent.astype(jnp.float32).reshape(count, -1, width)
    inverse = lax.rsqrt(jnp.mean(shaped * shaped, axis=2, keepdims=True) + 1e-06)
    inner = jnp.sum(weighted * shaped, axis=2, keepdims=True)
    result = weighted * inverse - shaped * inverse * inverse * inverse * inner / width
    return result.reshape(count, -1).astype(jnp.bfloat16)


def body(tokens, cotangent, drift, error, weight, momentum, factor, gain):
    replicas = lax.axis_size("replica")
    scale = 1.0 / math.sqrt(tokens.shape[1] * lax.axis_size("tensor"))
    merged = drift[0].astype(jnp.float32) + error[0].astype(jnp.float32)
    left = lax.psum(contract(factor, merged, 1, 1), ("replica", "tensor")) / replicas
    lower, ortho = factor_basis(left)
    new_factor = (
        lax.psum(contract(ortho, merged, 1, 0).astype(jnp.bfloat16), "replica").astype(jnp.float32)
        / replicas
    )
    approx = contract(ortho, new_factor, 0, 0)
    new_error = (merged - approx).astype(jnp.bfloat16)[None]
    own_count = weight.shape[0]
    offset = lax.axis_index("replica") * own_count
    own_approx = lax.dynamic_slice_in_dim(approx, offset, own_count, 0)
    new_momentum = outer_beta * momentum + own_approx
    new_weight = weight - outer_rate * (own_approx + outer_beta * new_momentum)
    rounded = new_weight.astype(jnp.bfloat16)
    partial_keys = (
        lax.dot_general(
            tokens,
            lax.all_gather(rounded, "replica", axis=0, tiled=True),
            (((1,), (1,)), ((), ())),
            preferred_element_type=jnp.float32,
        )
        * scale
    )
    keys = lax.psum(partial_keys.astype(jnp.bfloat16), "tensor").astype(jnp.float32)
    upstream = lax.all_gather(cotangent, "tensor", axis=0, tiled=True)
    grads = key_grad(keys, upstream, gain)
    summed = lax.dot_general(
        grads, tokens, (((0,), (0,)), ((), ())), preferred_element_type=jnp.float32
    )
    weight_grad = (summed * scale).astype(jnp.bfloat16)[None]
    return (new_weight, new_momentum, new_error, new_factor, weight_grad)


def solution(mesh):
    placed = (
        P("replica", "tensor"),
        P(("replica", "tensor"), None),
        P("replica", None, "tensor"),
        P("replica", None, "tensor"),
        P("replica", "tensor"),
        P("replica", "tensor"),
        P(None, "tensor"),
        P(),
    )
    return jax.shard_map(
        body,
        mesh=mesh,
        in_specs=placed,
        out_specs=(
            P("replica", "tensor"),
            P("replica", "tensor"),
            P("replica", None, "tensor"),
            P(None, "tensor"),
            P("replica", None, "tensor"),
        ),
        check_vma=False,
    )
```

profile of v0, /device:TPU:6, one launch (start us, length us, event | category | flops | bytes accessed | tf_op | source)
XLA Modules:
  0.0 758.8 jit_solution(8451883481890831862)
XLA Ops:
  7.2 0.0 copy-start
  7.2 0.0 all-reduce.3.cloned.1.call-start
  7.2 0.0 copy-start.1
  7.2 0.0 copy-start.2
  7.2 3.1 convolution_bitcast_fusion
  10.3 0.0 all-reduce.3.cloned.1.call-update
  10.4 0.0 all-reduce.5.cloned.1.call-start
  10.4 447.6 %all-reduce.3.cloned.1.call-done = f32[32,512]{1,0:T(8,128)} async-done(((f32[32,512]{1,0:T(8,128)}), f32[32,512]{1,0:T(8,128)}) %all-reduce.3.cloned.1.call-update) | async-done | bytes 65552 | tf_op jit(solution)/shard_map/psum | solution.py:45
  458.0 1.7 select_reduce_fusion.1
  459.7 0.0 copy-start.5
  459.7 0.1 copy.15
  460.4 2.9 cholesky.17
  463.4 0.6 compare_reduce_fusion
  464.0 0.7 fusion.22
  464.7 2.4 custom-call.7
  467.1 0.0 copy-done.5
  467.1 0.3 fusion.16
  467.4 0.0 copy-done.1
  467.4 0.0 copy-done.2
  467.4 0.8 convolution_convert_fusion
  468.2 113.1 %psum.22 = bf16[32,512]{1,0:T(8,128)(2,1)S(1)} all-reduce(bf16[32,512]{1,0:T(8,128)(2,1)S(1)} %convolution_convert_fusion), channel_id=1, replica_groups=mesh['replica'=32,'tensor'=16] {'replica'}, use_global_device_ids=true, to_apply=%region_4.5 | all-reduce | flops 16384 | bytes 65536 | tf_op jit(solution)/shard_map/psum | solution.py:48
  581.3 0.0 copy-start.4
  581.3 0.0 copy-start.7
  581.3 0.0 copy-start.8
  581.4 1.0 fusion.31
  582.4 0.0 copy-done.4
  582.4 0.0 copy-done.7
  582.4 0.0 copy-done.8
  582.4 0.6 fusion.28
  583.1 37.0 %all_gather.7 = bf16[512,512]{1,0:T(8,128)(2,1)S(1)} all-gather(bf16[16,512]{1,0:T(8,128)(2,1)S(1)} %get-tuple-element.5), channel_id=1, replica_groups=mesh['replica'=32,'tensor'=16] {'replica'}, dimensions={0}, use_global_device_ids=true | all-gather | bytes 540672 | tf_op jit(solution)/shard_map/all_gather | solution.py:62
  620.1 0.0 copy-done
  620.1 1.3 fusion.4
  621.4 0.0 copy-start.6
  621.4 0.0 all-reduce.5.cloned.1.call-update
  621.4 0.7 copy-done.6
  622.1 32.9 %all_gather.6 = bf16[512,512]{1,0:T(8,128)(2,1)} all-gather(bf16[32,512]{1,0:T(8,128)(2,1)S(1)} %copy-done.6), channel_id=1, replica_groups=mesh['replica'=32,'tensor'=16] {'tensor'}, dimensions={0}, use_global_device_ids=true | all-gather | bytes 557056 | tf_op jit(solution)/shard_map/all_gather | solution.py:69
  655.0 0.0 copy-start.9
  655.0 1.3 copy.16
  656.3 0.0 copy-done.9
  656.3 1.0 fusion.14
  657.3 91.4 %all-reduce.5.cloned.1.call-done = bf16[512,512]{0,1:T(8,128)(2,1)} async-done(((bf16[512,512]{0,1:T(8,128)(2,1)}), bf16[512,512]{0,1:T(8,128)(2,1)}) %all-reduce.5.cloned.1.call-update) | async-done | bytes 524304 | tf_op jit(solution)/shard_map/psum | solution.py:68
  748.7 0.0 copy-start.3
  748.7 1.2 multiply_reduce_fusion.1
  750.0 0.0 copy-done.3
  750.0 0.3 fusion
  750.3 0.4 fusion.6
  750.7 1.2 fusion.3
  (5 shorter events, 0.1 us)
Async XLA Ops:
  7.2 612.9 %copy-start = (bf16[512,512]{1,0:T(8,128)(2,1)S(1)}, bf16[512,512]{1,0:T(8,128)(2,1)}, u32[]{:S(2)}) copy-start(bf16[512,512]{1,0:T(8,128)(2,1)} %param.8) | copy-start | bytes 1572868
  7.2 450.8 %all-reduce.3.cloned.1.call-start = ((), (), s32[]{:S(2)}) async-start(), calls=%async_computation | async-start | bytes 131072 | tf_op jit(solution)/shard_map/psum | solution.py:45
  7.2 460.2 %copy-start.1 = (bf16[1,512,512]{2,1,0:T(8,128)(2,1)S(1)}, bf16[1,512,512]{2,1,0:T(8,128)(2,1)}, u32[]{:S(2)}) copy-start(bf16[1,512,512]{2,1,0:T(8,128)(2,1)} %param.11) | copy-start | bytes 1572868
  7.2 460.2 %copy-start.2 = (bf16[1,512,512]{2,1,0:T(8,128)(2,1)S(1)}, bf16[1,512,512]{2,1,0:T(8,128)(2,1)}, u32[]{:S(2)}) copy-start(bf16[1,512,512]{2,1,0:T(8,128)(2,1)} %param.10) | copy-start | bytes 1572868
  10.4 738.4 %all-reduce.5.cloned.1.call-start = ((), (), s32[]{:S(2)}) async-start(), calls=%async_computation.1 | async-start | bytes 1048576 | tf_op jit(solution)/shard_map/psum | solution.py:68
  459.7 7.4 copy-start.5
  581.3 1.1 copy-start.4
  581.3 1.1 copy-start.7
  581.3 1.1 copy-start.8
  621.4 0.8 copy-start.6
  655.0 1.3 copy-start.9
  748.7 1.3 copy-start.3
Sparse Core Ops, SparseCore 0:
  14.0 443.9 all-reduce.2
  621.5 127.1 all-reduce.4
where the time goes:
time: 759 us
  waiting for transfers between devices  539 us (71%)
  blocking collectives  183 us (24%)
  between operations  14.9 us (2%)
  other arithmetic  10.3 us (1%)
  matrix products  9.4 us (1%)
    psum x1, waiting for transfers between devices, body(): lax.psum(contract(factor, merged, 1, 1), ('replica', 'tensor')) / replicas  448 us
    psum x1, blocking collectives, body(): lax.psum(contract(ortho, merged, 1, 0).astype(jnp.bfloat16), 'replica')  113 us
    psum x1, waiting for transfers between devices, body(): lax.psum(partial_keys.astype(jnp.bfloat16), 'tensor').astype(jnp.float32)  91.4 us
    all_gather x1, blocking collectives, body(): lax.all_gather(rounded, 'replica', axis=0, tiled=True)  37 us
    all_gather x1, blocking collectives, body(): upstream = lax.all_gather(cotangent, 'tensor', axis=0, tiled=True)  32.9 us
  transfers between devices with their start and end apart: 2, of which 2 were waited for; matrix products, arithmetic and copies ran while one was open for 0% of the time, Pallas kernels for 0%

commit v1 on v0

v1 whole, which is shorter than its diff:
```python
import functools
import math

import jax
import jax.numpy as jnp
from jax import lax
from jax.experimental import pallas as pl
from jax.experimental.pallas import tpu as pltpu
from jax.sharding import PartitionSpec as P

MESH = pl.DeviceIdType.MESH
highest = lax.Precision.HIGHEST
f32 = jnp.float32
bf16 = jnp.bfloat16
outer_rate = 0.7
outer_beta = 0.9
LANES = 128
GROUP = 8


def dot(left, right, left_dim, right_dim, precision=None):
    return lax.dot_general(
        left,
        right,
        (((left_dim,), (right_dim,)), ((), ())),
        precision=precision,
        preferred_element_type=f32,
    )


def split_dot(left, right, left_dim, right_dim):
    high = left.astype(bf16)
    low = (left - high.astype(f32)).astype(bf16)
    return dot(high, right, left_dim, right_dim) + dot(low, right, left_dim, right_dim)


def send(src, dst, send_sem, recv_sem, device):
    pltpu.make_async_remote_copy(
        src_ref=src,
        dst_ref=dst,
        send_sem=send_sem,
        recv_sem=recv_sem,
        device_id=device,
        device_id_type=MESH,
    ).start()


def drain(ref, sem):
    pltpu.make_async_copy(ref, ref, sem).wait()


def each_other(count, me, act):
    def step(i, carry):
        half = (i + 1) // 2
        offset = count // 2 + half * (2 * (i % 2) - 1)
        act(lax.rem(me + offset, count))
        return carry

    lax.fori_loop(0, count - 1, step, 0)


def pack(rows, rank):
    groups = rows.shape[1] // GROUP
    total = rows[:, 0:GROUP]
    for g in range(1, groups):
        total = total + pltpu.roll(rows[:, g * GROUP : (g + 1) * GROUP], g * rank, 2)
    return total


def unpack(packed, groups, rank):
    lane = lax.broadcasted_iota(jnp.int32, packed.shape, 2)
    parts = []
    for g in range(groups):
        turned = packed if g == 0 else pltpu.roll(packed, LANES - g * rank, 2)
        parts.append(jnp.where(lane < rank, turned, 0.0))
    return jnp.concatenate(parts, axis=1)


def inverse_factor(gram, rank):
    row = lax.broadcasted_iota(jnp.int32, (rank, LANES), 0)
    lane = lax.broadcasted_iota(jnp.int32, (rank, LANES), 1)
    diagonal = row == lane
    trace = jnp.sum(
        jnp.sum(jnp.where(diagonal, gram, 0.0), axis=1, keepdims=True), axis=0, keepdims=True
    )
    shift = 0.001 * trace / rank + 1e-06
    a = jnp.where(lane < rank, gram, 0.0) + jnp.where(diagonal, shift, 0.0)
    a = a + jnp.where(lane == row + rank, 1.0, 0.0)
    down = lax.broadcasted_iota(jnp.int32, (rank, 1), 0)
    for k in range(rank - 1):
        pivot_row = a[k : k + 1, :]
        share = pivot_row * (1.0 / pivot_row[:, k : k + 1])
        column = jnp.where(down > k, a[:, k : k + 1], 0.0)
        a = a - column * share
    pivots = jnp.sum(jnp.where(diagonal, a, 0.0), axis=1, keepdims=True)
    a = a * (1.0 / jnp.sqrt(pivots))
    return jnp.where(lane < rank, pltpu.roll(a, LANES - rank, 1), 0.0)


def key_grad(keys, cotangent, gain):
    width = gain.shape[1]
    parts = []
    for head in range(keys.shape[1] // width):
        at = slice(head * width, (head + 1) * width)
        shaped = keys[:, at]
        weighted = gain * cotangent[:, at]
        inverse = lax.rsqrt(jnp.mean(shaped * shaped, axis=1, keepdims=True) + 1e-06)
        inner = jnp.sum(weighted * shaped, axis=1, keepdims=True)
        parts.append(
            weighted * inverse - shaped * (inverse * inverse * inverse * inner / width)
        )
    return jnp.concatenate(parts, axis=1)


def kernel(
    nr, nz, scale,
    tokens, cotangent, drift, error, weight, momentum, factor, gain,
    new_weight, new_momentum, new_error, new_factor, weight_grad,
    mb, pb, ps, mr, ub, mg, lz, la, lt, kb, kr, pp, pr, ga, ss, rs,
):
    r = lax.axis_index("replica")
    z = lax.axis_index("tensor")
    chips = nr // 2
    chip, core = r // 2, lax.rem(r, 2)
    other = 1 - core
    partner = {"replica": chip * 2 + other}
    rank, width = factor.shape
    keys = drift.shape[0]
    rows = weight.shape[0]
    mine = tokens.shape[0] // nz

    def across(chip_at):
        return {"replica": chip_at * 2 + core}

    barrier = pltpu.get_barrier_semaphore()

    def greet_replica(peer):
        pl.semaphore_signal(barrier, inc=1, device_id={"replica": peer}, device_id_type=MESH)

    def greet_tensor(peer):
        pl.semaphore_signal(barrier, inc=1, device_id={"tensor": peer}, device_id_type=MESH)

    each_other(nz, z, greet_tensor)
    each_other(nr, r, greet_replica)

    mb[...] = (drift[...].astype(f32) + error[...].astype(f32)).astype(bf16).reshape(mb.shape)
    base = weight[...] - (outer_rate * outer_beta * outer_beta) * momentum[...]
    ub[chip, core] = base.astype(bf16)
    pl.semaphore_wait(barrier, nr + nz - 2)

    send(mb.at[:, other], pb, ss.at[0], rs.at[0], partner)
    each_other(
        chips, chip,
        lambda p: send(ub.at[chip, core], ub.at[chip, core], ss.at[1], rs.at[1], across(p)),
    )
    drain(pb, rs.at[0])
    ps[...] = (mb[:, pl.ds(core, 1)][:, 0].astype(f32) + pb[...].astype(f32)).astype(bf16)
    each_other(
        chips, chip,
        lambda p: send(ps.at[p], mr.at[chip], ss.at[2], rs.at[2], across(p)),
    )
    mr[chip] = ps[chip]

    drain(ps.at[pl.ds(0, chips - 1)], rs.at[1])
    send(ub.at[:, core], ub.at[:, core], ss.at[3], rs.at[3], partner)

    drain(ps.at[pl.ds(0, chips - 1)], rs.at[2])
    mean = jnp.sum(mr[...].astype(f32), axis=0) * (1.0 / nr)
    padded = jnp.concatenate([factor[...], jnp.zeros((LANES - rank, width), f32)], axis=0)
    term = dot(mean, padded, 1, 1, highest)
    lz[z] = pack(term[None], rank)[0]
    each_other(
        nz, z,
        lambda p: send(lz.at[z], lz.at[z], ss.at[4], rs.at[4], {"tensor": p}),
    )
    mg[chip, core] = mean.astype(bf16)
    each_other(
        chips, chip,
        lambda p: send(mg.at[chip, core], mg.at[chip, core], ss.at[5], rs.at[5], across(p)),
    )

    drain(pb, rs.at[3])
    partial = dot(tokens[...], ub[...].reshape(keys, width), 1, 1) * scale
    kb[...] = partial.astype(bf16).reshape(kb.shape)
    each_other(
        nz, z,
        lambda p: send(kb.at[p], kr.at[z], ss.at[6], rs.at[6], {"tensor": p}),
    )
    kr[z] = kb[z]

    drain(ps.at[pl.ds(0, chips - 1)], rs.at[5])
    send(mg.at[:, core], mg.at[:, core], ss.at[7], rs.at[7], partner)

    drain(lz.at[pl.ds(0, nz - 1)], rs.at[4])
    la[r] = jnp.sum(lz[...], axis=0)
    each_other(
        nr, r,
        lambda p: send(la.at[r], la.at[r], ss.at[8], rs.at[8], {"replica": p}),
    )
    drain(pb, rs.at[7])
    drain(la.at[pl.ds(0, nr - 1)], rs.at[8])
    left = unpack(la[...], rows // GROUP, rank)
    lt[...] = left.reshape(lt.shape)
    left = left.reshape(keys, LANES)
    gram = dot(left, left, 0, 0, highest)[0:rank]
    inverse = inverse_factor(gram, rank)
    ortho = dot(inverse, left, 1, 1, highest)
    right = split_dot(ortho, mg[...].reshape(keys, width), 1, 0)
    new_factor[...] = right
    zeros = jnp.zeros((LANES - rank, width), f32)
    right_padded = jnp.concatenate([right, zeros], axis=0)
    product = dot(tokens[...], right_padded.astype(bf16), 1, 1)
    pp[...] = pack(product.reshape(nz, mine, LANES), rank)
    each_other(
        nz, z,
        lambda p: send(pp.at[p], pr.at[z], ss.at[9], rs.at[9], {"tensor": p}),
    )
    pr[z] = pp[z]

    inverse_padded = jnp.concatenate([inverse, jnp.zeros((LANES - rank, LANES), f32)], axis=0)
    own_ortho = dot(lt[r], inverse_padded, 1, 1, highest)
    own_approx = dot(own_ortho, right_padded, 1, 0, highest)
    next_momentum = outer_beta * momentum[...] + own_approx
    new_momentum[...] = next_momentum
    new_weight[...] = weight[...] - outer_rate * (own_approx + outer_beta * next_momentum)
    ortho_rows = dot(left, inverse_padded, 1, 1).astype(bf16)
    approx = dot(ortho_rows, right_padded.astype(bf16), 1, 0)
    merged = drift[...].astype(f32) + error[...].astype(f32)
    new_error[...] = (merged - approx).astype(bf16)

    drain(kb.at[pl.ds(0, nz - 1)], rs.at[6])
    base_keys = jnp.sum(kr[...].astype(f32), axis=0)
    drain(pp.at[pl.ds(0, nz - 1)], rs.at[9])
    summed = unpack(jnp.sum(pr[...], axis=0)[None], mine // GROUP, rank)[0]
    ortho_padded = jnp.concatenate([ortho, jnp.zeros((LANES - rank, keys), f32)], axis=0)
    turn = dot(summed, ortho_padded, 1, 0, highest)
    own_keys = base_keys - (outer_rate * (1.0 + outer_beta) * scale) * turn
    ga[z] = key_grad(own_keys, cotangent[...].astype(f32), gain[...]).astype(bf16)
    each_other(
        nz, z,
        lambda p: send(ga.at[z], ga.at[z], ss.at[10], rs.at[10], {"tensor": p}),
    )
    drain(ga.at[pl.ds(0, nz - 1)], rs.at[10])
    grads = ga[...].reshape(tokens.shape[0], keys)
    weight_grad[...] = (dot(grads, tokens[...], 0, 0) * scale).astype(bf16)

    drain(pb, ss.at[0])
    drain(ps.at[pl.ds(0, chips - 1)], ss.at[1])
    drain(ps.at[pl.ds(0, chips - 1)], ss.at[2])
    drain(pb, ss.at[3])
    drain(lz.at[pl.ds(0, nz - 1)], ss.at[4])
    drain(ps.at[pl.ds(0, chips - 1)], ss.at[5])
    drain(kb.at[pl.ds(0, nz - 1)], ss.at[6])
    drain(pb, ss.at[7])
    drain(la.at[pl.ds(0, nr - 1)], ss.at[8])
    drain(pp.at[pl.ds(0, nz - 1)], ss.at[9])
    drain(ga.at[pl.ds(0, nz - 1)], ss.at[10])


def solution(mesh):
    nr, nz = mesh.shape["replica"], mesh.shape["tensor"]
    chips = nr // 2

    def body(tokens, cotangent, drift, error, weight, momentum, factor, gain):
        count, width = tokens.shape
        keys = drift.shape[1]
        rows = weight.shape[0]
        mine = count // nz
        scale = 1.0 / math.sqrt(width * nz)
        shapes = (
            jax.ShapeDtypeStruct(weight.shape, f32),
            jax.ShapeDtypeStruct(weight.shape, f32),
            jax.ShapeDtypeStruct((keys, width), bf16),
            jax.ShapeDtypeStruct(factor.shape, f32),
            jax.ShapeDtypeStruct((keys, width), bf16),
        )
        in_vmem = pl.BlockSpec(memory_space=pltpu.VMEM)
        out = pl.pallas_call(
            functools.partial(kernel, nr, nz, scale),
            out_shape=shapes,
            in_specs=[in_vmem] * 8,
            out_specs=(in_vmem,) * 5,
            scratch_shapes=[
                pltpu.VMEM((chips, 2, rows, width), bf16),
                pltpu.VMEM((chips, rows, width), bf16),
                pltpu.VMEM((chips, rows, width), bf16),
                pltpu.VMEM((chips, rows, width), bf16),
                pltpu.VMEM((chips, 2, rows, width), bf16),
                pltpu.VMEM((chips, 2, rows, width), bf16),
                pltpu.VMEM((nz, GROUP, LANES), f32),
                pltpu.VMEM((nr, GROUP, LANES), f32),
                pltpu.VMEM((nr, rows, LANES), f32),
                pltpu.VMEM((nz, mine, keys), bf16),
                pltpu.VMEM((nz, mine, keys), bf16),
                pltpu.VMEM((nz, GROUP, LANES), f32),
                pltpu.VMEM((nz, GROUP, LANES), f32),
                pltpu.VMEM((nz, mine, keys), bf16),
                pltpu.SemaphoreType.DMA((11,)),
                pltpu.SemaphoreType.DMA((11,)),
            ],
            compiler_params=pltpu.CompilerParams(
                collective_id=0, has_side_effects=True, vmem_limit_bytes=40 * 1024 * 1024
            ),
            name="outer_inner_step",
        )(
            tokens, cotangent, drift[0], error[0], weight, momentum, factor, gain.reshape(1, -1)
        )
        return (out[0], out[1], out[2][None], out[3], out[4][None])

    placed = (
        P("replica", "tensor"),
        P(("replica", "tensor"), None),
        P("replica", None, "tensor"),
        P("replica", None, "tensor"),
        P("replica", "tensor"),
        P("replica", "tensor"),
        P(None, "tensor"),
        P(),
    )
    return jax.shard_map(
        body,
        mesh=mesh,
        in_specs=placed,
        out_specs=(
            P("replica", "tensor"),
            P("replica", "tensor"),
            P("replica", None, "tensor"),
            P(None, "tensor"),
            P("replica", None, "tensor"),
        ),
        check_vma=False,
    )
```

time: 759 us -> 93.6 us (0.12)
  waiting for transfers between devices: 539 us -> 0 us
  blocking collectives: 183 us -> 0 us
  Pallas kernels: 0 us -> 81 us
  between operations: 14.9 us -> 0.66 us
  other arithmetic: 10.3 us -> 0 us
  matrix products: 9.4 us -> 0 us
  local copies, waits for them, and re-layouts: 2.12 us -> 10.3 us
    psum x2 -> x0, waiting for transfers between devices: 539 us -> none  [the longest x1 448 us: body(): lax.psum(contract(factor, merged, 1, 1), ('replica', 'tensor')) / replicas]
    psum x1 -> x0, blocking collectives: 113 us -> none  [body(): lax.psum(contract(ortho, merged, 1, 0).astype(jnp.bfloat16), 'replica')]
    pallas_call x0 -> x1, Pallas kernels: none -> 81 us  [body(): pl.pallas_call(functools.partial(kernel, nr, nz, scale), out_shape=shapes...]
    all_gather x2 -> x0, blocking collectives: 69.9 us -> none  [the longest x1 37 us: body(): lax.all_gather(rounded, 'replica', axis=0, tiled=True)]
    unnamed x20 -> x21, local copies, waits for them, and re-layouts: 0.78 us -> 10.3 us
    dot_general x6 -> x0, matrix products: 9.12 us -> none  [the longest x4 6.63 us: contract(): lax.dot_general(left, right, (((left_dim,), (right_dim,)), ((), ())), pre...]
  transfers between devices with their start and end apart: 2 -> 0, of which waited for: 2 -> 0; matrix products, arithmetic and copies ran while one was open for 0% -> 0% of each run, Pallas kernels for 0% -> 0%
where the time goes in v1:
time: 93.6 us; the launch traced here: 92 us
  Pallas kernels  81 us (87%)
  local copies, waits for them, and re-layouts  10.3 us (11%)
    pallas_call x1, Pallas kernels, body(): pl.pallas_call(functools.partial(kernel, nr, nz, scale), out_shape=shapes...  81 us
    unnamed x21, local copies, waits for them, and re-layouts  10.3 us

profile of v1, /device:TPU:6, one launch (start us, length us, event | category | flops | bytes accessed | tf_op | source)
XLA Modules:
  0.0 92.0 jit_solution(12668325658589664017)
XLA Ops:
  0.6 0.0 copy-start.7
  0.6 0.6 copy-done.7
  1.3 0.0 copy-start
  1.3 1.0 %copy-done = bf16[512,512]{1,0:T(8,128)(2,1)S(1)} copy-done((bf16[512,512]{1,0:T(8,128)(2,1)S(1)}, bf16[512,512]{1,0:T(8,128)(2,1)}, u32[]{:S(2)}) %copy-start) | copy-done | bytes 524312
  2.3 0.0 copy-start.1
  2.3 1.0 %copy-done.1 = bf16[1,512,512]{2,1,0:T(8,128)(2,1)S(1)} copy-done((bf16[1,512,512]{2,1,0:T(8,128)(2,1)S(1)}, bf16[1,512,512]{2,1,0:T(8,128)(2,1)}, u32[]{:S(2)}) %copy-start.1) | copy-done | bytes 524312
  3.4 0.0 copy-start.2
  3.4 1.0 %copy-done.2 = bf16[1,512,512]{2,1,0:T(8,128)(2,1)S(1)} copy-done((bf16[1,512,512]{2,1,0:T(8,128)(2,1)S(1)}, bf16[1,512,512]{2,1,0:T(8,128)(2,1)}, u32[]{:S(2)}) %copy-start.2) | copy-done | bytes 524312
  4.4 0.0 copy-start.3
  4.4 0.8 copy-done.3
  5.3 0.0 copy-start.4
  5.3 0.8 copy-done.4
  6.0 0.0 copy-start.5
  6.0 0.8 copy-done.5
  6.8 0.0 copy-start.6
  6.8 0.8 copy-done.6
  7.5 81.0 %outer_inner_step.1 = (f32[16,512]{1,0:T(8,128)S(1)}, f32[16,512]{1,0:T(8,128)S(1)}, bf16[512,512]{1,0:T(8,128)(2,1)S(1)}, f32[32,512]{1,0:T(8,128)S(1)}, bf16[512,512]{1,0:T(8,128)(2,1)S(1)}) custom-call(bf16[512,512]{1,0:T(8,128)(2,1)S(1)} %copy-done, bf16[32,512]{1,0:T(8,128)(2,1)S(1)} %copy-done.4, bf16[512,512]{1,0:T(8,128)(2,1)S(1)} %bitcast.5, ...), custom_call_target="tpu_custom_call" | custom-call | tf_op jit(solution)/shard_map/outer_inner_step/pallas_call | solution.py:278
  88.5 0.6 copy.18
  89.2 0.6 copy.19
  89.8 0.8 copy.20
  90.6 0.6 copy.21
  91.2 0.8 copy.22
Async XLA Ops:
  0.6 0.7 copy-start.7
  1.3 1.0 %copy-start = (bf16[512,512]{1,0:T(8,128)(2,1)S(1)}, bf16[512,512]{1,0:T(8,128)(2,1)}, u32[]{:S(2)}) copy-start(bf16[512,512]{1,0:T(8,128)(2,1)} %tokens.1) | copy-start | bytes 1572868
  2.3 1.0 %copy-start.1 = (bf16[1,512,512]{2,1,0:T(8,128)(2,1)S(1)}, bf16[1,512,512]{2,1,0:T(8,128)(2,1)}, u32[]{:S(2)}) copy-start(bf16[1,512,512]{2,1,0:T(8,128)(2,1)} %param.10) | copy-start | bytes 1572868
  3.4 1.0 %copy-start.2 = (bf16[1,512,512]{2,1,0:T(8,128)(2,1)S(1)}, bf16[1,512,512]{2,1,0:T(8,128)(2,1)}, u32[]{:S(2)}) copy-start(bf16[1,512,512]{2,1,0:T(8,128)(2,1)} %param.11) | copy-start | bytes 1572868
  4.4 0.8 copy-start.3
  5.3 0.8 copy-start.4
  6.0 0.8 copy-start.5
  6.8 0.8 copy-start.6

commit v2 on v1

--- a/solution.py
+++ b/solution.py
@@ -16,6 +16,7 @@
 outer_beta = 0.9
 LANES = 128
 GROUP = 8
+GRANT = 60 * 1024 * 1024
 
 
 def dot(left, right, left_dim, right_dim, precision=None):
@@ -112,11 +113,119 @@
     return jnp.concatenate(parts, axis=1)
 
 
+def gather_ring(count, me, ga, ss, rs, at):
+    half = ga.shape[1] // 2
+
+    def peer(offset):
+        return {"tensor": lax.rem(me + offset + count, count)}
+
+    def block(offset):
+        return ga.at[lax.rem(me + offset + count, count)]
+
+    near = at + 2
+    send(block(0), block(0), ss.at[at], rs.at[at], peer(5))
+    send(block(0), block(0), ss.at[at + 1], rs.at[at + 1], peer(-5))
+    for offset in (2, -2, 1, -1):
+        send(block(0), block(0), ss.at[near], rs.at[near], peer(offset))
+    drain(block(0), rs.at[at])
+    low = block(-5).at[pl.ds(0, half)]
+    send(low, low, ss.at[near], rs.at[near], peer(3))
+    for offset in (2, -2, 1, -1):
+        send(block(-5), block(-5), ss.at[near], rs.at[near], peer(offset))
+    drain(block(0), rs.at[at + 1])
+    high = block(5).at[pl.ds(half, half)]
+    send(high, high, ss.at[near], rs.at[near], peer(-3))
+    for offset in (2, -2, 1, -1):
+        send(block(5), block(5), ss.at[near], rs.at[near], peer(offset))
+    drain(ga.at[pl.ds(0, 13)], rs.at[near])
+    drain(block(0), ss.at[at])
+    drain(block(0), ss.at[at + 1])
+    drain(ga.at[pl.ds(0, 13)], ss.at[near])
+
+
+def scatter_near(count, me, kb, kn, kh, ss, rs, at):
+    half = kb.shape[1] // 2
+
+    def index(offset):
+        return lax.rem(me + offset + 2 * count, count)
+
+    for far, offset in ((5, 3), (-5, -3)):
+        side = 0 if far > 0 else 1
+        send(
+            kb.at[index(offset + far), pl.ds(side * half, half)], kh.at[side],
+            ss.at[at], rs.at[at], {"tensor": index(offset)},
+        )
+    for i, far in enumerate((5, -5, 0)):
+        for j, offset in enumerate((2, -2, 1, -1)):
+            send(
+                kb.at[index(offset + far)], kn.at[j, i],
+                ss.at[at], rs.at[at], {"tensor": index(offset)},
+            )
+
+
+def scatter_far(count, me, kb, kn, kh, ks, kr, ss, rs, at):
+    half = kb.shape[1] // 2
+
+    def index(offset):
+        return lax.rem(me + offset + 2 * count, count)
+
+    drain(kb.at[pl.ds(0, 13)], rs.at[at])
+    for i, far in enumerate((5, -5)):
+        total = kb[index(far)].astype(f32)
+        for j in range(4):
+            total = total + kn[j, i].astype(f32)
+        eighth = kh[i].astype(f32)
+        blank = jnp.zeros_like(eighth)
+        total = total + jnp.concatenate([eighth, blank] if i == 0 else [blank, eighth], axis=0)
+        ks[i] = total.astype(bf16)
+        send(ks.at[i], kr.at[i], ss.at[at + 1], rs.at[at + 1], {"tensor": index(far)})
+    total = kb[me].astype(f32)
+    for j in range(4):
+        total = total + kn[j, 2].astype(f32)
+    return total
+
+
+def finish(
+    scale, nw_at, nm_at, ne_at, nf_at, tokens_at, grads_at,
+    nw_out, nm_out, ne_out, nf_out, wg_out,
+    nw, nm, ne, nf, tokens, grads, held, in_sems, out_sems,
+):
+    pairs = (
+        (grads_at, grads), (tokens_at, tokens),
+        (ne_at, ne), (nf_at, nf), (nw_at, nw), (nm_at, nm),
+    )
+    ins = [pltpu.make_async_copy(src, dst, in_sems.at[i]) for i, (src, dst) in enumerate(pairs)]
+    for copy in ins:
+        copy.start()
+    outs = []
+
+    def leave(src, dst):
+        outs.append(pltpu.make_async_copy(src, dst, out_sems.at[len(outs)]))
+        outs[-1].start()
+
+    ins[0].wait()
+    ins[1].wait()
+    half = held.shape[1]
+    for i in range(2):
+        left = grads[:, i * half : (i + 1) * half]
+        held[i] = (dot(left, tokens[...], 0, 0) * scale).astype(bf16)
+        leave(held.at[i], wg_out.at[pl.ds(i * half, half)])
+        if i == 0:
+            results = ((ne, ne_out), (nf, nf_out), (nw, nw_out), (nm, nm_out))
+            for load, (src, dst) in zip(ins[2:], results):
+                load.wait()
+                leave(src, dst)
+    for copy in outs:
+        copy.wait()
+
+
 def kernel(
     nr, nz, scale,
+    tokens_at, cotangent_at, drift_at, error_at, weight_at, momentum_at, factor_at, gain_at,
+    new_weight_at, new_momentum_at, new_error_at, new_factor_at, grads_at,
+    new_weight, new_momentum, new_error, new_factor, ga,
     tokens, cotangent, drift, error, weight, momentum, factor, gain,
-    new_weight, new_momentum, new_error, new_factor, weight_grad,
-    mb, pb, ps, mr, ub, mg, lz, la, lt, kb, kr, pp, pr, ga, ss, rs,
+    mb, pb, ps, mr, ub, mg, lz, la, lt, kb, kn, kh, ks, kr, pp, pr, ss, rs, ls,
 ):
     r = lax.axis_index("replica")
     z = lax.axis_index("tensor")
@@ -132,6 +241,23 @@
     def across(chip_at):
         return {"replica": chip_at * 2 + core}
 
+    loads = [
+        pltpu.make_async_copy(src, dst, ls.at[i])
+        for i, (src, dst) in enumerate(
+            (
+                (drift_at, drift),
+                (error_at, error),
+                (weight_at, weight),
+                (momentum_at, momentum),
+                (factor_at, factor),
+                (tokens_at, tokens),
+                (cotangent_at, cotangent),
+                (gain_at, gain),
+            )
+        )
+    ]
+    for load in loads[:4]:
+        load.start()
     barrier = pltpu.get_barrier_semaphore()
 
     def greet_replica(peer):
@@ -142,22 +268,28 @@
 
     each_other(nz, z, greet_tensor)
     each_other(nr, r, greet_replica)
+    for load in loads[4:]:
+        load.start()
+    for load in loads[:4]:
+        load.wait()
 
     mb[...] = (drift[...].astype(f32) + error[...].astype(f32)).astype(bf16).reshape(mb.shape)
     base = weight[...] - (outer_rate * outer_beta * outer_beta) * momentum[...]
     ub[chip, core] = base.astype(bf16)
+    for load in loads[4:]:
+        load.wait()
     pl.semaphore_wait(barrier, nr + nz - 2)
 
     send(mb.at[:, other], pb, ss.at[0], rs.at[0], partner)
-    each_other(
-        chips, chip,
-        lambda p: send(ub.at[chip, core], ub.at[chip, core], ss.at[1], rs.at[1], across(p)),
-    )
     drain(pb, rs.at[0])
     ps[...] = (mb[:, pl.ds(core, 1)][:, 0].astype(f32) + pb[...].astype(f32)).astype(bf16)
     each_other(
         chips, chip,
         lambda p: send(ps.at[p], mr.at[chip], ss.at[2], rs.at[2], across(p)),
+    )
+    each_other(
+        chips, chip,
+        lambda p: send(ub.at[chip, core], ub.at[chip, core], ss.at[1], rs.at[1], across(p)),
     )
     mr[chip] = ps[chip]
 
@@ -182,11 +314,7 @@
     drain(pb, rs.at[3])
     partial = dot(tokens[...], ub[...].reshape(keys, width), 1, 1) * scale
     kb[...] = partial.astype(bf16).reshape(kb.shape)
-    each_other(
-        nz, z,
-        lambda p: send(kb.at[p], kr.at[z], ss.at[6], rs.at[6], {"tensor": p}),
-    )
-    kr[z] = kb[z]
+    scatter_near(nz, z, kb, kn, kh, ss, rs, 13)
 
     drain(ps.at[pl.ds(0, chips - 1)], rs.at[5])
     send(mg.at[:, core], mg.at[:, core], ss.at[7], rs.at[7], partner)
@@ -197,6 +325,7 @@
         nr, r,
         lambda p: send(la.at[r], la.at[r], ss.at[8], rs.at[8], {"replica": p}),
     )
+    near_keys = scatter_far(nz, z, kb, kn, kh, ks, kr, ss, rs, 13)
     drain(pb, rs.at[7])
     drain(la.at[pl.ds(0, nr - 1)], rs.at[8])
     left = unpack(la[...], rows // GROUP, rank)
@@ -228,21 +357,31 @@
     merged = drift[...].astype(f32) + error[...].astype(f32)
     new_error[...] = (merged - approx).astype(bf16)
 
-    drain(kb.at[pl.ds(0, nz - 1)], rs.at[6])
-    base_keys = jnp.sum(kr[...].astype(f32), axis=0)
+    stores = [
+        pltpu.make_async_copy(src, dst, ls.at[i])
+        for i, (src, dst) in enumerate(
+            (
+                (new_error, new_error_at),
+                (new_factor, new_factor_at),
+                (new_weight, new_weight_at),
+                (new_momentum, new_momentum_at),
+            )
+        )
+    ]
+    for store in stores:
+        store.start()
+
+    drain(kr, rs.at[14])
+    base_keys = near_keys + kr[0].astype(f32) + kr[1].astype(f32)
     drain(pp.at[pl.ds(0, nz - 1)], rs.at[9])
     summed = unpack(jnp.sum(pr[...], axis=0)[None], mine // GROUP, rank)[0]
     ortho_padded = jnp.concatenate([ortho, jnp.zeros((LANES - rank, keys), f32)], axis=0)
     turn = dot(summed, ortho_padded, 1, 0, highest)
     own_keys = base_keys - (outer_rate * (1.0 + outer_beta) * scale) * turn
     ga[z] = key_grad(own_keys, cotangent[...].astype(f32), gain[...]).astype(bf16)
-    each_other(
-        nz, z,
-        lambda p: send(ga.at[z], ga.at[z], ss.at[10], rs.at[10], {"tensor": p}),
-    )
-    drain(ga.at[pl.ds(0, nz - 1)], rs.at[10])
-    grads = ga[...].reshape(tokens.shape[0], keys)
-    weight_grad[...] = (dot(grads, tokens[...], 0, 0) * scale).astype(bf16)
+    gather_ring(nz, z, ga, ss, rs, 10)
+    last = pltpu.make_async_copy(ga, grads_at, ls.at[4])
+    last.start()
 
     drain(pb, ss.at[0])
     drain(ps.at[pl.ds(0, chips - 1)], ss.at[1])
@@ -250,11 +389,14 @@
     drain(pb, ss.at[3])
     drain(lz.at[pl.ds(0, nz - 1)], ss.at[4])
     drain(ps.at[pl.ds(0, chips - 1)], ss.at[5])
-    drain(kb.at[pl.ds(0, nz - 1)], ss.at[6])
+    drain(kb.at[pl.ds(0, 13)], ss.at[13])
+    drain(ks, ss.at[14])
     drain(pb, ss.at[7])
     drain(la.at[pl.ds(0, nr - 1)], ss.at[8])
     drain(pp.at[pl.ds(0, nz - 1)], ss.at[9])
-    drain(ga.at[pl.ds(0, nz - 1)], ss.at[10])
+    for store in stores:
+        store.wait()
+    last.wait()
 
 
 def solution(mesh):
@@ -267,20 +409,36 @@
         rows = weight.shape[0]
         mine = count // nz
         scale = 1.0 / math.sqrt(width * nz)
-        shapes = (
-            jax.ShapeDtypeStruct(weight.shape, f32),
-            jax.ShapeDtypeStruct(weight.shape, f32),
-            jax.ShapeDtypeStruct((keys, width), bf16),
-            jax.ShapeDtypeStruct(factor.shape, f32),
-            jax.ShapeDtypeStruct((keys, width), bf16),
-        )
+        state = jax.ShapeDtypeStruct(weight.shape, f32)
+        square = jax.ShapeDtypeStruct((keys, width), bf16)
+        right = jax.ShapeDtypeStruct(factor.shape, f32)
         in_vmem = pl.BlockSpec(memory_space=pltpu.VMEM)
-        out = pl.pallas_call(
+        in_hbm = pl.BlockSpec(memory_space=pltpu.HBM)
+        held = pl.pallas_call(
             functools.partial(kernel, nr, nz, scale),
-            out_shape=shapes,
-            in_specs=[in_vmem] * 8,
-            out_specs=(in_vmem,) * 5,
+            out_shape=(
+                state,
+                state,
+                square,
+                right,
+                jax.ShapeDtypeStruct((nz, mine, keys), bf16),
+            ),
+            in_specs=[in_hbm] * 8,
+            out_specs=(in_hbm,) * 5,
             scratch_shapes=[
+                pltpu.VMEM(weight.shape, f32),
+                pltpu.VMEM(weight.shape, f32),
+                pltpu.VMEM((keys, width), bf16),
+                pltpu.VMEM(factor.shape, f32),
+                pltpu.VMEM((nz, mine, keys), bf16),
+                pltpu.VMEM(tokens.shape, bf16),
+                pltpu.VMEM(cotangent.shape, bf16),
+                pltpu.VMEM((keys, width), bf16),
+                pltpu.VMEM((keys, width), bf16),
+                pltpu.VMEM(weight.shape, f32),
+                pltpu.VMEM(weight.shape, f32),
+                pltpu.VMEM(factor.shape, f32),
+                pltpu.VMEM((1, LANES), f32),
                 pltpu.VMEM((chips, 2, rows, width), bf16),
                 pltpu.VMEM((chips, rows, width), bf16),
                 pltpu.VMEM((chips, rows, width), bf16),
@@ -291,20 +449,42 @@
                 pltpu.VMEM((nr, GROUP, LANES), f32),
                 pltpu.VMEM((nr, rows, LANES), f32),
                 pltpu.VMEM((nz, mine, keys), bf16),
-                pltpu.VMEM((nz, mine, keys), bf16),
+                pltpu.VMEM((4, 3, mine, keys), bf16),
+                pltpu.VMEM((2, mine // 2, keys), bf16),
+                pltpu.VMEM((2, mine, keys), bf16),
+                pltpu.VMEM((2, mine, keys), bf16),
                 pltpu.VMEM((nz, GROUP, LANES), f32),
                 pltpu.VMEM((nz, GROUP, LANES), f32),
-                pltpu.VMEM((nz, mine, keys), bf16),
-                pltpu.SemaphoreType.DMA((11,)),
-                pltpu.SemaphoreType.DMA((11,)),
+                pltpu.SemaphoreType.DMA((15,)),
+                pltpu.SemaphoreType.DMA((15,)),
+                pltpu.SemaphoreType.DMA((8,)),
             ],
             compiler_params=pltpu.CompilerParams(
-                collective_id=0, has_side_effects=True, vmem_limit_bytes=40 * 1024 * 1024
+                collective_id=0, has_side_effects=True, vmem_limit_bytes=GRANT
             ),
             name="outer_inner_step",
         )(
             tokens, cotangent, drift[0], error[0], weight, momentum, factor, gain.reshape(1, -1)
         )
+        out = pl.pallas_call(
+            functools.partial(finish, scale),
+            out_shape=(state, state, square, right, square),
+            in_specs=[in_hbm] * 6,
+            out_specs=(in_hbm,) * 5,
+            scratch_shapes=[
+                pltpu.VMEM(weight.shape, f32),
+                pltpu.VMEM(weight.shape, f32),
+                pltpu.VMEM((keys, width), bf16),
+                pltpu.VMEM(factor.shape, f32),
+                pltpu.VMEM((count, width), bf16),
+                pltpu.VMEM((count, keys), bf16),
+                pltpu.VMEM((2, keys // 2, width), bf16),
+                pltpu.SemaphoreType.DMA((6,)),
+                pltpu.SemaphoreType.DMA((6,)),
+            ],
+            compiler_params=pltpu.CompilerParams(vmem_limit_bytes=GRANT),
+            name="weight_gradient",
+        )(*held[:4], tokens, held[4].reshape(count, keys))
         return (out[0], out[1], out[2][None], out[3], out[4][None])
 
     placed = (

time: 93.6 us -> 69.7 us (0.74)
  the two profiles are of different devices: /device:TPU:6 before, /device:TPU:32 now
where the time goes in v2:
time: 69.7 us; the launch traced here: 69.5 us
  Pallas kernels  68.9 us (99%)
    pallas_call x1, Pallas kernels, body(): pl.pallas_call(functools.partial(kernel, nr, nz, scale), out_shape=(state...  66.2 us
    pallas_call x1, Pallas kernels, body(): pl.pallas_call(functools.partial(finish, scale), out_shape=(state, state,...  2.66 us

profile of v2, /device:TPU:32, one launch (start us, length us, event | category | flops | bytes accessed | tf_op | source)
XLA Modules:
  0.0 69.5 jit_solution(16328830127301628867)
XLA Ops:
  0.6 66.2 %outer_inner_step.1 = (f32[16,512]{1,0:T(8,128)}, f32[16,512]{1,0:T(8,128)}, bf16[512,512]{1,0:T(8,128)(2,1)}, f32[32,512]{1,0:T(8,128)}, bf16[16,32,512]{2,1,0:T(8,128)(2,1)}) custom-call(bf16[512,512]{1,0:T(8,128)(2,1)} %tokens_at.3, bf16[32,512]{1,0:T(8,128)(2,1)} %cotangent_at.1, bf16[512,512]{1,0:T(8,128)(2,1)} %bitcast.6, bf16[512,512]{1,0:T(8,128)(2,1)} %bitcast.7, ...), custom_call_target="tpu_custom_call" | custom-call | tf_op jit(solution)/shard_map/outer_inner_step/pallas_call | solution.py:417
  66.9 2.7 %weight_gradient.1 = (f32[16,512]{1,0:T(8,128)}, f32[16,512]{1,0:T(8,128)}, bf16[512,512]{1,0:T(8,128)(2,1)}, f32[32,512]{1,0:T(8,128)}, bf16[512,512]{1,0:T(8,128)(2,1)}) custom-call(f32[16,512]{1,0:T(8,128)} %get-tuple-element.15.nw_at, f32[16,512]{1,0:T(8,128)} %get-tuple-element.16.nm_at, bf16[512,512]{1,0:T(8,128)(2,1)} %get-tuple-element.17.ne_at, ...), custom_call_target="tpu_custom_call" | custom-call | tf_op jit(solution)/shard_map/weight_gradient/pallas_call | solution.py:469

commit v3 on v2

--- a/solution.py
+++ b/solution.py
@@ -57,7 +57,7 @@
         act(lax.rem(me + offset, count))
         return carry
 
-    lax.fori_loop(0, count - 1, step, 0)
+    lax.fori_loop(0, count - 1, step, 0, unroll=True)
 
 
 def pack(rows, rank):
@@ -75,6 +75,15 @@
         turned = packed if g == 0 else pltpu.roll(packed, LANES - g * rank, 2)
         parts.append(jnp.where(lane < rank, turned, 0.0))
     return jnp.concatenate(parts, axis=1)
+
+
+def fold(packed):
+    turned = pltpu.roll(pltpu.roll(packed, LANES // 2, 2), GROUP // 2, 1)
+    return (packed + turned)[:, 0 : GROUP // 2]
+
+
+def unfold(folded):
+    return jnp.concatenate([folded, pltpu.roll(folded, LANES // 2, 2)], axis=1)
 
 
 def inverse_factor(gram, rank):
@@ -225,7 +234,7 @@
     new_weight_at, new_momentum_at, new_error_at, new_factor_at, grads_at,
     new_weight, new_momentum, new_error, new_factor, ga,
     tokens, cotangent, drift, error, weight, momentum, factor, gain,
-    mb, pb, ps, mr, ub, mg, lz, la, lt, kb, kn, kh, ks, kr, pp, pr, ss, rs, ls,
+    mb, pb, ps, mr, ub, mg, lp, lq, lz, la, lt, kb, kn, kh, ks, kr, pp, pr, ss, rs, ls,
 ):
     r = lax.axis_index("replica")
     z = lax.axis_index("tensor")
@@ -273,38 +282,47 @@
     for load in loads[:4]:
         load.wait()
 
-    mb[...] = (drift[...].astype(f32) + error[...].astype(f32)).astype(bf16).reshape(mb.shape)
+    merged = drift[...].astype(f32) + error[...].astype(f32)
+    mb[...] = merged.astype(bf16).reshape(mb.shape)
     base = weight[...] - (outer_rate * outer_beta * outer_beta) * momentum[...]
     ub[chip, core] = base.astype(bf16)
     for load in loads[4:]:
         load.wait()
+    padded = jnp.concatenate([factor[...], jnp.zeros((LANES - rank, width), f32)], axis=0)
+    term = dot(merged, padded, 1, 1, highest) * (1.0 / nr)
+    lp[...] = fold(pack(term.reshape(nr, rows, LANES), rank))
     pl.semaphore_wait(barrier, nr + nz - 2)
 
+    each_other(
+        nr, r,
+        lambda p: send(lp.at[p], lq.at[r], ss.at[15], rs.at[15], {"replica": p}),
+    )
+    lq[r] = lp[r]
+
     send(mb.at[:, other], pb, ss.at[0], rs.at[0], partner)
+    each_other(
+        chips, chip,
+        lambda p: send(ub.at[chip, core], ub.at[chip, core], ss.at[1], rs.at[1], across(p)),
+    )
     drain(pb, rs.at[0])
     ps[...] = (mb[:, pl.ds(core, 1)][:, 0].astype(f32) + pb[...].astype(f32)).astype(bf16)
     each_other(
         chips, chip,
         lambda p: send(ps.at[p], mr.at[chip], ss.at[2], rs.at[2], across(p)),
     )
-    each_other(
-        chips, chip,
-        lambda p: send(ub.at[chip, core], ub.at[chip, core], ss.at[1], rs.at[1], across(p)),
-    )
     mr[chip] = ps[chip]
+
+    drain(lq.at[pl.ds(0, nr - 1)], rs.at[15])
+    lz[z] = jnp.sum(lq[...], axis=0)
+    each_other(
+        nz, z,
+        lambda p: send(lz.at[z], lz.at[z], ss.at[4], rs.at[4], {"tensor": p}),
+    )
 
     drain(ps.at[pl.ds(0, chips - 1)], rs.at[1])
     send(ub.at[:, core], ub.at[:, core], ss.at[3], rs.at[3], partner)
-
     drain(ps.at[pl.ds(0, chips - 1)], rs.at[2])
     mean = jnp.sum(mr[...].astype(f32), axis=0) * (1.0 / nr)
-    padded = jnp.concatenate([factor[...], jnp.zeros((LANES - rank, width), f32)], axis=0)
-    term = dot(mean, padded, 1, 1, highest)
-    lz[z] = pack(term[None], rank)[0]
-    each_other(
-        nz, z,
-        lambda p: send(lz.at[z], lz.at[z], ss.at[4], rs.at[4], {"tensor": p}),
-    )
     mg[chip, core] = mean.astype(bf16)
     each_other(
         chips, chip,
@@ -316,19 +334,18 @@
     kb[...] = partial.astype(bf16).reshape(kb.shape)
     scatter_near(nz, z, kb, kn, kh, ss, rs, 13)
 
+    drain(lz.at[pl.ds(0, nz - 1)], rs.at[4])
+    la[r] = jnp.sum(lz[...], axis=0)
+    each_other(
+        nr, r,
+        lambda p: send(la.at[r], la.at[r], ss.at[8], rs.at[8], {"replica": p}),
+    )
     drain(ps.at[pl.ds(0, chips - 1)], rs.at[5])
     send(mg.at[:, core], mg.at[:, core], ss.at[7], rs.at[7], partner)
-
-    drain(lz.at[pl.ds(0, nz - 1)], rs.at[4])
-    la[r] = jnp.sum(lz[...], axis=0)
-    each_other(
-        nr, r,
-        lambda p: send(la.at[r], la.at[r], ss.at[8], rs.at[8], {"replica": p}),
-    )
     near_keys = scatter_far(nz, z, kb, kn, kh, ks, kr, ss, rs, 13)
     drain(pb, rs.at[7])
     drain(la.at[pl.ds(0, nr - 1)], rs.at[8])
-    left = unpack(la[...], rows // GROUP, rank)
+    left = unpack(unfold(la[...]), rows // GROUP, rank)
     lt[...] = left.reshape(lt.shape)
     left = left.reshape(keys, LANES)
     gram = dot(left, left, 0, 0, highest)[0:rank]
@@ -354,7 +371,6 @@
     new_weight[...] = weight[...] - outer_rate * (own_approx + outer_beta * next_momentum)
     ortho_rows = dot(left, inverse_padded, 1, 1).astype(bf16)
     approx = dot(ortho_rows, right_padded.astype(bf16), 1, 0)
-    merged = drift[...].astype(f32) + error[...].astype(f32)
     new_error[...] = (merged - approx).astype(bf16)
 
     stores = [
@@ -393,6 +409,7 @@
     drain(ks, ss.at[14])
     drain(pb, ss.at[7])
     drain(la.at[pl.ds(0, nr - 1)], ss.at[8])
+    drain(lq.at[pl.ds(0, nr - 1)], ss.at[15])
     drain(pp.at[pl.ds(0, nz - 1)], ss.at[9])
     for store in stores:
         store.wait()
@@ -445,8 +462,10 @@
                 pltpu.VMEM((chips, rows, width), bf16),
                 pltpu.VMEM((chips, 2, rows, width), bf16),
                 pltpu.VMEM((chips, 2, rows, width), bf16),
-                pltpu.VMEM((nz, GROUP, LANES), f32),
-                pltpu.VMEM((nr, GROUP, LANES), f32),
+                pltpu.VMEM((nr, GROUP // 2, LANES), f32),
+                pltpu.VMEM((nr, GROUP // 2, LANES), f32),
+                pltpu.VMEM((nz, GROUP // 2, LANES), f32),
+                pltpu.VMEM((nr, GROUP // 2, LANES), f32),
                 pltpu.VMEM((nr, rows, LANES), f32),
                 pltpu.VMEM((nz, mine, keys), bf16),
                 pltpu.VMEM((4, 3, mine, keys), bf16),
@@ -455,8 +474,8 @@
                 pltpu.VMEM((2, mine, keys), bf16),
                 pltpu.VMEM((nz, GROUP, LANES), f32),
                 pltpu.VMEM((nz, GROUP, LANES), f32),
-                pltpu.SemaphoreType.DMA((15,)),
-                pltpu.SemaphoreType.DMA((15,)),
+                pltpu.SemaphoreType.DMA((16,)),
+                pltpu.SemaphoreType.DMA((16,)),
                 pltpu.SemaphoreType.DMA((8,)),
             ],
             compiler_params=pltpu.CompilerParams(

time: 69.7 us -> 64.6 us (0.927)
  the two profiles are of different devices: /device:TPU:32 before, /device:TPU:6 now
where the time goes in v3:
time: 64.6 us; the launch traced here: 64.4 us
  Pallas kernels  63.7 us (99%)
    pallas_call x1, Pallas kernels, body(): pl.pallas_call(functools.partial(kernel, nr, nz, scale), out_shape=(state...  61.1 us
    pallas_call x1, Pallas kernels, body(): pl.pallas_call(functools.partial(finish, scale), out_shape=(state, state,...  2.67 us

profile of v3, /device:TPU:6, one launch (start us, length us, event | category | flops | bytes accessed | tf_op | source)
XLA Modules:
  0.0 64.4 jit_solution(11489311010496434603)
XLA Ops:
  0.6 61.1 %outer_inner_step.1 = (f32[16,512]{1,0:T(8,128)}, f32[16,512]{1,0:T(8,128)}, bf16[512,512]{1,0:T(8,128)(2,1)}, f32[32,512]{1,0:T(8,128)}, bf16[16,32,512]{2,1,0:T(8,128)(2,1)}) custom-call(bf16[512,512]{1,0:T(8,128)(2,1)} %tokens_at.3, bf16[32,512]{1,0:T(8,128)(2,1)} %cotangent_at.1, bf16[512,512]{1,0:T(8,128)(2,1)} %bitcast.6, bf16[512,512]{1,0:T(8,128)(2,1)} %bitcast.7, ...), custom_call_target="tpu_custom_call" | custom-call | tf_op jit(solution)/shard_map/outer_inner_step/pallas_call | solution.py:434
  61.7 2.7 %weight_gradient.1 = (f32[16,512]{1,0:T(8,128)}, f32[16,512]{1,0:T(8,128)}, bf16[512,512]{1,0:T(8,128)(2,1)}, f32[32,512]{1,0:T(8,128)}, bf16[512,512]{1,0:T(8,128)(2,1)}) custom-call(f32[16,512]{1,0:T(8,128)} %get-tuple-element.15.nw_at, f32[16,512]{1,0:T(8,128)} %get-tuple-element.16.nm_at, bf16[512,512]{1,0:T(8,128)(2,1)} %get-tuple-element.17.ne_at, ...), custom_call_target="tpu_custom_call" | custom-call | tf_op jit(solution)/shard_map/weight_gradient/pallas_call | solution.py:488

commit v4 on v3

--- a/solution.py
+++ b/solution.py
@@ -97,11 +97,16 @@
     a = jnp.where(lane < rank, gram, 0.0) + jnp.where(diagonal, shift, 0.0)
     a = a + jnp.where(lane == row + rank, 1.0, 0.0)
     down = lax.broadcasted_iota(jnp.int32, (rank, 1), 0)
-    for k in range(rank - 1):
-        pivot_row = a[k : k + 1, :]
-        share = pivot_row * (1.0 / pivot_row[:, k : k + 1])
-        column = jnp.where(down > k, a[:, k : k + 1], 0.0)
-        a = a - column * share
+    for k in range(0, rank, 2):
+        first, second = a[k : k + 1, :], a[k + 1 : k + 2, :]
+        corner, cross, last = first[:, k : k + 1], first[:, k + 1 : k + 2], second[:, k + 1 : k + 2]
+        scaled = 1.0 / corner
+        ratio = cross * scaled
+        share = 1.0 / (last - cross * ratio)
+        second = second - ratio * first
+        near = jnp.where(down > k, a[:, k : k + 1], 0.0)
+        far = jnp.where(down > k + 1, a[:, k + 1 : k + 2] - ratio * near, 0.0)
+        a = a - near * (first * scaled) - far * (second * share)
     pivots = jnp.sum(jnp.where(diagonal, a, 0.0), axis=1, keepdims=True)
     a = a * (1.0 / jnp.sqrt(pivots))
     return jnp.where(lane < rank, pltpu.roll(a, LANES - rank, 1), 0.0)
@@ -164,7 +169,7 @@
             kb.at[index(offset + far), pl.ds(side * half, half)], kh.at[side],
             ss.at[at], rs.at[at], {"tensor": index(offset)},
         )
-    for i, far in enumerate((5, -5, 0)):
+    for i, far in enumerate((5, -5)):
         for j, offset in enumerate((2, -2, 1, -1)):
             send(
                 kb.at[index(offset + far)], kn.at[j, i],
@@ -178,7 +183,7 @@
     def index(offset):
         return lax.rem(me + offset + 2 * count, count)
 
-    drain(kb.at[pl.ds(0, 13)], rs.at[at])
+    drain(kb.at[pl.ds(0, 9)], rs.at[at])
     for i, far in enumerate((5, -5)):
         total = kb[index(far)].astype(f32)
         for j in range(4):
@@ -188,10 +193,11 @@
         total = total + jnp.concatenate([eighth, blank] if i == 0 else [blank, eighth], axis=0)
         ks[i] = total.astype(bf16)
         send(ks.at[i], kr.at[i], ss.at[at + 1], rs.at[at + 1], {"tensor": index(far)})
-    total = kb[me].astype(f32)
-    for j in range(4):
-        total = total + kn[j, 2].astype(f32)
-    return total
+    for j, offset in enumerate((2, -2, 1, -1)):
+        send(
+            kb.at[index(offset)], kn.at[j, 2],
+            ss.at[at], rs.at[at + 3], {"tensor": index(offset)},
+        )
 
 
 def finish(
@@ -342,7 +348,7 @@
     )
     drain(ps.at[pl.ds(0, chips - 1)], rs.at[5])
     send(mg.at[:, core], mg.at[:, core], ss.at[7], rs.at[7], partner)
-    near_keys = scatter_far(nz, z, kb, kn, kh, ks, kr, ss, rs, 13)
+    scatter_far(nz, z, kb, kn, kh, ks, kr, ss, rs, 13)
     drain(pb, rs.at[7])
     drain(la.at[pl.ds(0, nr - 1)], rs.at[8])
     left = unpack(unfold(la[...]), rows // GROUP, rank)
@@ -388,7 +394,10 @@
         store.start()
 
     drain(kr, rs.at[14])
-    base_keys = near_keys + kr[0].astype(f32) + kr[1].astype(f32)
+    drain(kb.at[pl.ds(0, 4)], rs.at[16])
+    base_keys = kb[z].astype(f32) + kr[0].astype(f32) + kr[1].astype(f32)
+    for j in range(4):
+        base_keys = base_keys + kn[j, 2].astype(f32)
     drain(pp.at[pl.ds(0, nz - 1)], rs.at[9])
     summed = unpack(jnp.sum(pr[...], axis=0)[None], mine // GROUP, rank)[0]
     ortho_padded = jnp.concatenate([ortho, jnp.zeros((LANES - rank, keys), f32)], axis=0)
@@ -474,8 +483,8 @@
                 pltpu.VMEM((2, mine, keys), bf16),
                 pltpu.VMEM((nz, GROUP, LANES), f32),
                 pltpu.VMEM((nz, GROUP, LANES), f32),
-                pltpu.SemaphoreType.DMA((16,)),
-                pltpu.SemaphoreType.DMA((16,)),
+                pltpu.SemaphoreType.DMA((17,)),
+                pltpu.SemaphoreType.DMA((17,)),
                 pltpu.SemaphoreType.DMA((8,)),
             ],
             compiler_params=pltpu.CompilerParams(

time: 64.6 us -> 63.3 us (0.980)
  Pallas kernels: 63.7 us -> 62.5 us
    pallas_call x1, Pallas kernels: 61.1 us -> 59.8 us  [body(): pl.pallas_call(functools.partial(kernel, nr, nz, scale), out_shape=(state...]
where the time goes in v4:
time: 63.3 us; the launch traced here: 63.1 us
  Pallas kernels  62.5 us (99%)
  between operations  0.64 us (1%)
    pallas_call x1, Pallas kernels, body(): pl.pallas_call(functools.partial(kernel, nr, nz, scale), out_shape=(state...  59.8 us
    pallas_call x1, Pallas kernels, body(): pl.pallas_call(functools.partial(finish, scale), out_shape=(state, state,...  2.67 us

profile of v4, /device:TPU:6, one launch (start us, length us, event | category | flops | bytes accessed | tf_op | source)
XLA Modules:
  0.0 63.1 jit_solution(5756449573605298150)
XLA Ops:
  0.6 59.8 %outer_inner_step.1 = (f32[16,512]{1,0:T(8,128)}, f32[16,512]{1,0:T(8,128)}, bf16[512,512]{1,0:T(8,128)(2,1)}, f32[32,512]{1,0:T(8,128)}, bf16[16,32,512]{2,1,0:T(8,128)(2,1)}) custom-call(bf16[512,512]{1,0:T(8,128)(2,1)} %tokens_at.3, bf16[32,512]{1,0:T(8,128)(2,1)} %cotangent_at.1, bf16[512,512]{1,0:T(8,128)(2,1)} %bitcast.6, bf16[512,512]{1,0:T(8,128)(2,1)} %bitcast.7, ...), custom_call_target="tpu_custom_call" | custom-call | tf_op jit(solution)/shard_map/outer_inner_step/pallas_call | solution.py:443
  60.4 2.7 %weight_gradient.1 = (f32[16,512]{1,0:T(8,128)}, f32[16,512]{1,0:T(8,128)}, bf16[512,512]{1,0:T(8,128)(2,1)}, f32[32,512]{1,0:T(8,128)}, bf16[512,512]{1,0:T(8,128)(2,1)}) custom-call(f32[16,512]{1,0:T(8,128)} %get-tuple-element.15.nw_at, f32[16,512]{1,0:T(8,128)} %get-tuple-element.16.nm_at, bf16[512,512]{1,0:T(8,128)(2,1)} %get-tuple-element.17.ne_at, ...), custom_call_target="tpu_custom_call" | custom-call | tf_op jit(solution)/shard_map/weight_gradient/pallas_call | solution.py:497
